TPU v7x, 512 devices: a whole 4x4x16 slice. The times are simulated.
512 devices in a mesh: wide: 64 (over z, x_hi, core), narrow: 8 (over y, x_lo).
Axes of the slice: x: 4 (x_hi: 2, x_lo: 2; x = x_hi * 2 + x_lo), y: 4, z: 16, core: 2. Of those that a mesh axis runs over, the one named last changes fastest.
Arguments:
- panels: bfloat16 [64, 8192, 128], P('wide', 'narrow'), may hold values from -6 to 6
- stiff_blocks: bfloat16 [64, 1216, 4096], P('wide', 'narrow'), may hold values from -0.375 to 0.375
- mass_blocks: bfloat16 [64, 1216, 4096], P('wide', 'narrow'), may hold values from -0.375 to 0.375
- block_rows: int32 [64, 1216], P('wide', 'narrow'), may hold values from 0 to 16, as said below
- block_cols: int32 [64, 1216], P('wide', 'narrow'), may hold values from 0 to 127
- interface_map: int32 [64, 8192], P('wide', 'narrow'), may hold values from 0 to 8191, as said below
- cond_vectors: bfloat16 [8192, 768], P('narrow'), may hold values from -0.1875 to 0.1875
Outputs:
- condensed: bfloat16 [64, 8, 768, 512], P('wide', 'narrow')
Inputs may be any that keep to these rules, and one draw needn't show every extreme that they name: `block_rows`: in each partition's 152 slots the used slots come first; on some partition all 152 are used. `interface_map`: for every cell a permutation of the rows; of the 1024 rows of one partition at most 256 land in any one interface group, and in every cell some partition sends exactly 256 to some group.
All inputs are finite; a program needn't handle non-finite values.
Results may differ from a plain program's by a relative error of at most 0.0049.
Values may be sent and summed in bfloat16 or wider, within the bound.
A program may use at most 128 MiB of HBM per device.

v0:
```python
import jax
import jax.numpy as jnp
from jax import lax
from jax.sharding import PartitionSpec as P

BLK = 64
PC = 128
NC = 768
RB_DEV = 16
ROWS_DEV = 1024


def from_root(value, axis, source):
    kept = jnp.where(lax.axis_index(axis) == source, value, 0).astype(value.dtype)
    return lax.psum(kept, axis)


def body(panels, stiff_blocks, mass_blocks, block_rows, block_cols, interface_map, cond_vectors):
    group_count = lax.axis_size("narrow")
    cell_count = lax.axis_size("wide")
    slot_count = block_rows.shape[1]
    cell_blocks = RB_DEV * group_count
    peer_cap = 2 * ROWS_DEV // group_count
    stiffness = stiff_blocks.reshape(slot_count, BLK, BLK)
    mass_matrix = mass_blocks.reshape(slot_count, BLK, BLK)
    row_index = block_rows.reshape(slot_count)
    column_index = block_cols.reshape(slot_count)
    selector = (row_index[None, :] == jnp.arange(RB_DEV)[:, None]).astype(jnp.float32)
    owners = (0, cell_count // 2)
    panel_list = []
    for owner_index in owners:
        owner_rows = from_root(panels, "wide", owner_index)
        panel_list.append(lax.all_gather(owner_rows, "narrow", axis=1, tiled=True))
    pieces = []
    for panel_whole in panel_list:
        blocks = panel_whole.reshape(cell_blocks, BLK, PC)[column_index]
        for matrix in (stiffness, mass_matrix):
            product = jnp.einsum("sij,sjc->sic", matrix, blocks, preferred_element_type=jnp.float32)
            summed = jnp.einsum("rs,sic->ric", selector, product, precision=lax.Precision.HIGHEST)
            pieces.append(summed.reshape(ROWS_DEV, PC))
    product_rows = jnp.concatenate(pieces, axis=1).astype(jnp.bfloat16)
    position = interface_map.reshape(ROWS_DEV)
    target = position // ROWS_DEV
    slot_index = position % ROWS_DEV
    target_hits = (target[:, None] == jnp.arange(group_count)[None, :]).astype(jnp.int32)
    bucket_rank = jnp.sum(jnp.cumsum(target_hits, axis=0) * target_hits, axis=1) - 1
    send_rows = (
        jnp.zeros((group_count, peer_cap, 4 * PC), jnp.bfloat16)
        .at[target, bucket_rank]
        .set(product_rows)
    )
    send_slots = (
        jnp.full((group_count, peer_cap), ROWS_DEV, jnp.int32)
        .at[target, bucket_rank]
        .set(slot_index)
    )
    arrived, arrived_slots = (
        lax.all_to_all(send_rows, "narrow", split_axis=0, concat_axis=0, tiled=True),
        lax.all_to_all(send_slots, "narrow", split_axis=0, concat_axis=0, tiled=True),
    )
    placed = (
        jnp.zeros((ROWS_DEV, 4 * PC), jnp.bfloat16)
        .at[arrived_slots.reshape(-1)]
        .set(arrived.reshape(-1, 4 * PC), mode="drop")
    )
    condensed = lax.dot_general(
        cond_vectors, placed, (((0,), (0,)), ((), ())), preferred_element_type=jnp.float32
    )
    return condensed.astype(jnp.bfloat16).reshape(1, 1, NC, 4 * PC)


def solution(mesh):
    return jax.shard_map(
        body,
        mesh=mesh,
        in_specs=(
            P("wide", "narrow", None),
            P("wide", "narrow", None),
            P("wide", "narrow", None),
            P("wide", "narrow"),
            P("wide", "narrow"),
            P("wide", "narrow"),
            P("narrow", None),
        ),
        out_specs=P("wide", "narrow", None, None),
        check_vma=False,
    )
```

profile of v0, /device:TPU:1, one launch (start us, length us, event | category | flops | bytes accessed | tf_op | source)
XLA Modules:
  0.0 748.8 jit_solution(6269135097737931937)
XLA Ops:
  6.5 0.0 copy-start
  6.5 0.0 copy-start.5
  6.5 0.0 all-reduce.3.cloned.1.call-start
  6.5 1.9 broadcast_select_fusion.1
  8.5 0.0 all-reduce.3.cloned.1.call-update
  8.5 0.0 all-gather.3.cloned.1.call-start
  8.5 532.3 %all-reduce.3.cloned.1.call-done = (bf16[1,1024,128]{2,1,0:T(8,128)(2,1)}, bf16[1,1024,128]{2,1,0:T(8,128)(2,1)}) async-done(((bf16[1,1024,128]{2,1,0:T(8,128)(2,1)}, bf16[1,1024,128]{2,1,0:T(8,128)(2,1)}), (bf16[1,1024,128]{2,1,0:T(8,128)(2,1)}, bf16[1,1024,128]{2,1,0:T(8,128)(2,1)})) %all-reduce.3.cloned.1.call-update) | async-done | bytes 524304 | tf_op jit(solution)/shard_map/psum | solution.py:15
  540.8 0.0 all-gather.3.cloned.1.call-update
  540.9 0.0 all-gather.5.cloned.1.call-start
  540.9 0.7 all-gather.5.cloned.1.call-update
  541.6 0.7 add_select_fusion.1
  542.3 2.3 reduce-window.6
  544.6 0.3 slice_reduce_fusion
  544.8 0.2 reduce-window.9
  545.0 0.7 add_select_fusion
  545.7 0.1 add_bitcast_fusion
  545.8 0.7 compare_select_fusion.1
  546.5 0.7 multiply_reduce_fusion
  547.3 0.8 and_reduce_fusion
  548.0 4.9 scatter_custom_fusion.1
  552.9 4.0 all-to-all-start
  556.9 0.0 copy-done.5
  557.0 4.1 reshape.241
  561.0 0.0 copy-start.7
  561.0 4.8 reshape.243
  565.8 0.0 copy-done.7
  565.8 35.7 %all-gather.3.cloned.1.call-done = bf16[1,8192,128]{2,1,0:T(8,128)(2,1)} async-done(((bf16[1,1024,128]{2,1,0:T(8,128)(2,1)}), bf16[1,8192,128]{2,1,0:T(8,128)(2,1)}) %all-gather.3.cloned.1.call-update) | async-done | bytes 2097168 | tf_op jit(solution)/shard_map/all_gather | solution.py:33
  601.5 4.1 gather_fusion
  605.6 0.0 copy-start.1
  605.6 0.0 copy-start.4
  605.6 5.6 fusion.54
  611.2 0.0 copy-done.1
  611.2 0.0 copy-done.4
  611.2 3.0 fusion.55
  614.3 48.6 %all-gather.5.cloned.1.call-done = bf16[1,8192,128]{2,1,0:T(8,128)(2,1)} async-done(((bf16[1,1024,128]{2,1,0:T(8,128)(2,1)}), bf16[1,8192,128]{2,1,0:T(8,128)(2,1)}) %all-gather.5.cloned.1.call-update) | async-done | bytes 2097168 | tf_op jit(solution)/shard_map/all_gather | solution.py:33
  662.9 4.0 gather_fusion.1
  666.9 0.0 copy-start.2
  666.9 0.0 copy-start.3
  667.0 0.0 slice-start.2
  667.0 3.4 fusion.56
  670.4 0.0 copy-done.2
  670.4 0.5 copy-done.3
  670.9 0.8 fusion.57
  671.7 0.4 slice-done.2
  672.1 1.6 slice-done.3
  673.8 0.0 copy-done.6
  673.8 4.5 fusion.13
  678.3 0.0 slice-done
  678.3 0.0 slice-done.1
  678.3 4.7 fusion.16
  683.1 4.5 fusion.19
  687.6 4.5 fusion.22
  692.1 0.1 copy.9
  692.2 0.1 copy.10
  692.3 0.1 copy.11
  692.3 0.1 copy.12
  692.4 7.0 scatter_custom_fusion.2
  699.4 0.0 all-to-all-done
  699.4 4.3 all-to-all-start.1
  703.8 26.1 %all-to-all-done.1 = bf16[8,256,512]{2,1,0:T(8,128)(2,1)} async-done(((bf16[8,256,512]{2,1,0:T(8,128)(2,1)}), bf16[8,256,512]{2,1,0:T(8,128)(2,1)}, u32[]{:S(2)}, u32[]{:S(2)}) %all-to-all-start.1) | async-done | bytes 2097184 | tf_op jit(solution)/shard_map/all_to_all | solution.py:58
  729.9 10.2 %scatter_custom_fusion = bf16[1024,512]{1,0:T(8,128)(2,1)S(1)} fusion(s32[2048]{0:T(1024)S(1)} %bitcast.105, bf16[2048,512]{1,0:T(8,128)(2,1)} %bitcast.24, bf16[]{:T(256)} %constant.46.clone.1), kind=kCustom, calls=%fused_computation.32 | custom fusion | bytes 1049088 | tf_op jit(solution)/shard_map/scatter | solution.py:64
  740.1 0.0 copy-done
  740.1 1.0 fusion.12
  741.1 1.2 copy.13
  (13 shorter events, 0.1 us)
Async XLA Ops:
  6.5 733.6 %copy-start = (bf16[1024,768]{1,0:T(8,128)(2,1)S(1)}, bf16[1024,768]{1,0:T(8,128)(2,1)}, u32[]{:S(2)}) copy-start(bf16[1024,768]{1,0:T(8,128)(2,1)} %param.13) | copy-start | bytes 4718596
  6.5 550.4 %copy-start.5 = (bf16[1,152,4096]{2,1,0:T(8,128)(2,1)S(1)}, bf16[1,152,4096]{2,1,0:T(8,128)(2,1)}, u32[]{:S(2)}) copy-start(bf16[1,152,4096]{2,1,0:T(8,128)(2,1)} %param.8) | copy-start | bytes 3735556
  6.5 534.3 %all-reduce.3.cloned.1.call-start = ((), (), s32[]{:S(2)}) async-start(), calls=%async_computation.4 | async-start | bytes 1048576 | tf_op jit(solution)/shard_map/psum | solution.py:15
  8.5 593.0 %all-gather.3.cloned.1.call-start = ((), (), s32[]{:S(2)}) async-start(), calls=%async_computation.2 | async-start | bytes 2359296 | tf_op jit(solution)/shard_map/all_gather | solution.py:33
  540.9 122.0 %all-gather.5.cloned.1.call-start = ((), (), s32[]{:S(2)}) async-start(), calls=%async_computation.3 | async-start | bytes 2359296 | tf_op jit(solution)/shard_map/all_gather | solution.py:33
  552.9 146.5 %all-to-all-start = ((s32[8,1,256]{2,1,0:T(1,128)}), s32[8,1,256]{2,1,0:T(1,128)S(1)}, u32[]{:S(2)}, u32[]{:S(2)}) async-start(s32[8,1,256]{2,1,0:T(1,128)} %bitcast.6), calls=%async_computation | async-start | bytes 16384 | tf_op jit(solution)/shard_map/all_to_all | solution.py:59
  561.0 4.8 copy-start.7
  605.6 5.6 copy-start.1
  605.6 5.6 copy-start.4
  666.9 3.4 copy-start.2
  666.9 3.9 copy-start.3
  667.0 5.2 slice-start.2
  667.0 11.3 %slice-start = ((s8[4980736]{0:T(1024)(128)(4,1)}), s8[4194304]{0:T(1024)(128)(4,1)S(1)}, s32[]{:S(2)}) async-start(s8[4980736]{0:T(1024)(128)(4,1)} %bitcast.84), calls=%async_computation.5 | async-start | bytes 8388608
  670.9 2.9 slice-start.3
  670.9 2.9 copy-start.6
  670.9 7.4 slice-start.1
  699.4 30.5 %all-to-all-start.1 = ((bf16[8,256,512]{2,1,0:T(8,128)(2,1)}), bf16[8,256,512]{2,1,0:T(8,128)(2,1)}, u32[]{:S(2)}, u32[]{:S(2)}) async-start(bf16[8,256,512]{2,1,0:T(8,128)(2,1)} %bitcast.88), calls=%async_computation.1 | async-start | bytes 4194304 | tf_op jit(solution)/shard_map/all_to_all | solution.py:58
Sparse Core Ops, SparseCore 0:
  10.3 530.4 all-reduce.2
  543.1 58.3 all-gather.2
  603.8 59.0 all-gather.4
where the time goes:
time: 749 us
  waiting for transfers between devices  643 us (86%)
  local copies, waits for them, and re-layouts  36.4 us (5%)
  matrix products  32.2 us (4%)
  other arithmetic  15.1 us (2%)
  between operations  13.3 us (2%)
  starting transfers between devices  8.44 us (1%)
    psum x1, waiting for transfers between devices, from_root(): return lax.psum(kept, axis)  532 us
    all_gather x2, waiting for transfers between devices, body(): panel_list.append(lax.all_gather(owner_rows, 'narrow', axis=1, tiled=True))  84.3 us
    all_to_all x1, waiting for transfers between devices, body(): lax.all_to_all(send_rows, 'narrow', split_axis=0, concat_axis=0, tiled=True)  26.1 us
    dot_general x4, matrix products, body(): jnp.einsum('rs,sic->ric', selector, product, precision=lax.Precision.HIGH...  18.3 us
  transfers between devices with their start and end apart: 5, of which 4 were waited for; matrix products, arithmetic and copies ran while one was open for 9% of the time, Pallas kernels for 0%

commit v1 on v0

--- a/solution.py
+++ b/solution.py
@@ -2,6 +2,7 @@
 import jax.numpy as jnp
 from jax import lax
 from jax.sharding import PartitionSpec as P
+from jax.lax import all_gather
 
 BLK = 64
 PC = 128
@@ -12,7 +13,13 @@
 
 def from_root(value, axis, source):
     kept = jnp.where(lax.axis_index(axis) == source, value, 0).astype(value.dtype)
-    return lax.psum(kept, axis)
+
+    def group_matrix(mine_x):
+        arr_next = all_gather(mine_x, axis)
+        state_next = jnp.sum(arr_next, axis=0)
+        return state_next
+
+    return group_matrix(kept)
 
 
 def body(panels, stiff_blocks, mass_blocks, block_rows, block_cols, interface_map, cond_vectors):

time: 749 us -> 614 us (0.82)
  waiting for transfers between devices: 643 us -> 495 us
  other arithmetic: 15.1 us -> 30.6 us
    psum x1 -> x0, waiting for transfers between devices: 532 us -> none  [from_root(): return lax.psum(kept, axis)]
    all_gather x0 -> x2, waiting for transfers between devices: none -> 385 us  [group_matrix(): arr_next = all_gather(mine_x, axis)]
    reduce_sum x0 -> x2, other arithmetic: none -> 19 us  [group_matrix(): state_next = jnp.sum(arr_next, axis=0)]
  transfers between devices with their start and end apart: 5 -> 6, of which waited for: 4 -> 5; matrix products, arithmetic and copies ran while one was open for 9% -> 12% of each run, Pallas kernels for 0% -> 0%
where the time goes in v1:
time: 614 us; the launch traced here: 609 us
  waiting for transfers between devices  495 us (81%)
  local copies, waits for them, and re-layouts  36.7 us (6%)
  other arithmetic  30.6 us (5%)
  matrix products  25.1 us (4%)
  between operations  13.6 us (2%)
  starting transfers between devices  8.51 us (1%)
    all_gather x2, waiting for transfers between devices, group_matrix(): arr_next = all_gather(mine_x, axis)  385 us
    all_gather x2, waiting for transfers between devices, body(): panel_list.append(lax.all_gather(owner_rows, 'narrow', axis=1, tiled=True))  82.5 us
    all_to_all x1, waiting for transfers between devices, body(): lax.all_to_all(send_rows, 'narrow', split_axis=0, concat_axis=0, tiled=True)  26.1 us
    reduce_sum x2, other arithmetic, group_matrix(): state_next = jnp.sum(arr_next, axis=0)  19 us
    dot_general x4, matrix products, body(): jnp.einsum('rs,sic->ric', selector, product, precision=lax.Precision.HIGH...  18.3 us
  transfers between devices with their start and end apart: 6, of which 5 were waited for; matrix products, arithmetic and copies ran while one was open for 12% of the time, Pallas kernels for 0%

profile of v1, /device:TPU:1, one launch (start us, length us, event | category | flops | bytes accessed | tf_op | source)
XLA Modules:
  0.0 609.3 jit_solution(3030305789585106457)
XLA Ops:
  6.5 0.0 copy-start
  6.5 0.0 all-gather.13.cloned.1.call-start
  6.5 1.9 broadcast_select_fusion.1
  8.4 0.0 all-gather.13.cloned.1.call-update
  8.5 0.0 all-gather.9.cloned.1.call-start
  8.5 0.7 all-gather.9.cloned.1.call-update
  9.2 0.0 all-gather.15.cloned.1.call-start
  9.3 202.1 %all-gather.13.cloned.1.call-done = bf16[64,1024,128]{2,1,0:T(8,128)(2,1)} async-done(((bf16[1,1024,128]{2,1,0:T(8,128)(2,1)}), bf16[64,1024,128]{2,1,0:T(8,128)(2,1)}) %all-gather.13.cloned.1.call-update) | async-done | bytes 16777232 | tf_op jit(solution)/shard_map/all_gather | solution.py:18
  211.4 9.5 %reduce.9 = bf16[1024,128]{1,0:T(8,128)(2,1)} reduce(bf16[64,1024,128]{2,1,0:T(8,128)(2,1)} %all-gather.13.cloned.1.call-done, bf16[]{:T(256)} %constant.49.clone.1), dimensions={0}, to_apply=%region_5.6 | reduce | flops 8257536 | bytes 17039362 | tf_op jit(solution)/shard_map/reduce_sum | solution.py:19
  220.9 0.0 all-gather.15.cloned.1.call-update
  220.9 0.0 copy-start.6
  220.9 0.0 copy-start.10
  220.9 0.0 copy-start.9
  220.9 0.0 copy-start.5
  220.9 0.0 all-gather.11.cloned.1.call-start
  221.0 183.3 %all-gather.9.cloned.1.call-done = bf16[64,1024,128]{2,1,0:T(8,128)(2,1)} async-done(((bf16[1,1024,128]{2,1,0:T(8,128)(2,1)}), bf16[64,1024,128]{2,1,0:T(8,128)(2,1)}) %all-gather.9.cloned.1.call-update) | async-done | bytes 16777232 | tf_op jit(solution)/shard_map/all_gather | solution.py:18
  404.3 9.5 %reduce.8 = bf16[1024,128]{1,0:T(8,128)(2,1)} reduce(bf16[64,1024,128]{2,1,0:T(8,128)(2,1)} %all-gather.9.cloned.1.call-done, bf16[]{:T(256)} %constant.49.clone.1), dimensions={0}, to_apply=%region_4.5 | reduce | flops 8257536 | bytes 17039362 | tf_op jit(solution)/shard_map/reduce_sum | solution.py:19
  413.8 0.0 all-gather.11.cloned.1.call-update
  413.8 0.0 copy-done.6
  413.8 2.3 reduce-window.6
  416.1 0.3 slice_reduce_fusion
  416.4 0.2 reduce-window.9
  416.6 0.1 add_bitcast_fusion
  416.7 0.0 copy-done.10
  416.7 0.1 multiply_reduce_fusion
  416.8 0.0 copy-done.9
  416.8 0.1 and_reduce_fusion
  416.9 4.9 scatter_custom_fusion.1
  421.8 4.0 all-to-all-start
  425.8 0.0 copy-done.5
  425.8 4.1 reshape.243
  429.9 0.0 copy-start.8
  429.9 5.2 reshape.245
  435.1 0.0 copy-done.8
  435.1 25.5 %all-gather.15.cloned.1.call-done = bf16[8192,128]{1,0:T(8,128)(2,1)} async-done(((bf16[1024,128]{1,0:T(8,128)(2,1)}), bf16[8192,128]{1,0:T(8,128)(2,1)}) %all-gather.15.cloned.1.call-update) | async-done | bytes 2097168 | tf_op jit(solution)/shard_map/all_gather | solution.py:40
  460.6 4.1 gather_fusion.1
  464.7 57.0 %all-gather.11.cloned.1.call-done = bf16[8192,128]{1,0:T(8,128)(2,1)} async-done(((bf16[1024,128]{1,0:T(8,128)(2,1)}), bf16[8192,128]{1,0:T(8,128)(2,1)}) %all-gather.11.cloned.1.call-update) | async-done | bytes 2097168 | tf_op jit(solution)/shard_map/all_gather | solution.py:40
  521.7 4.1 gather_fusion
  525.9 0.0 copy-start.2
  525.9 3.4 convolution_bitcast_fusion.2
  529.3 0.0 copy-done.2
  529.3 0.5 copy-done.4
  529.8 0.8 convolution_bitcast_fusion.3
  530.6 0.9 copy-done.3
  531.5 0.8 convolution_bitcast_fusion.1
  532.3 0.9 copy-done.1
  533.2 0.8 convolution_bitcast_fusion
  534.0 0.0 copy-done.7
  534.0 4.5 fusion.12
  538.6 4.7 fusion.9
  543.3 4.5 fusion.15
  547.8 4.5 fusion.18
  552.3 0.1 copy.17
  552.4 0.1 copy.15
  552.5 0.1 copy.19
  552.5 0.1 copy.21
  552.6 7.0 %scatter_custom_fusion.2 = bf16[2048,512]{1,0:T(8,128)(2,1)} fusion(s32[1024]{0:T(1024)S(1)} %broadcast_select_fusion.2, bf16[1024,128]{1,0:T(8,128)(2,1)S(1)} %bitcast.81, bf16[]{:T(256)} %constant.84, bf16[1024,128]{1,0:T(8,128)(2,1)S(1)} %bitcast.80, bf16[1024,128]{1,0:T(8,128)(2,1)S(1)} %bitcast.78, bf16[1024,128]{1,0:T(8,128)(2,1)S(1)} %bitcast.79, ...), kind=kCustom, calls=%fused_computation.23 | custom fusion | flops 4194304 | bytes 3145732
  559.6 0.0 all-to-all-done
  559.6 4.4 all-to-all-start.1
  564.0 26.1 %all-to-all-done.1 = bf16[8,256,512]{2,1,0:T(8,128)(2,1)} async-done(((bf16[8,256,512]{2,1,0:T(8,128)(2,1)}), bf16[8,256,512]{2,1,0:T(8,128)(2,1)}, u32[]{:S(2)}, u32[]{:S(2)}) %all-to-all-start.1) | async-done | bytes 2097184 | tf_op jit(solution)/shard_map/all_to_all | solution.py:65
  590.1 10.2 %scatter_custom_fusion = bf16[1024,512]{1,0:T(8,128)(2,1)S(1)} fusion(s32[2048]{0:T(1024)S(1)} %bitcast.92, bf16[2048,512]{1,0:T(8,128)(2,1)} %bitcast.24, bf16[]{:T(256)} %constant.49.clone.1), kind=kCustom, calls=%fused_computation.32 | custom fusion | bytes 1049088 | tf_op jit(solution)/shard_map/scatter | solution.py:71
  600.3 0.0 copy-done
  600.3 1.0 fusion.8
  601.4 1.2 copy.22
  (14 shorter events, 0.1 us)
Async XLA Ops:
  6.5 593.8 %copy-start = (bf16[1024,768]{1,0:T(8,128)(2,1)S(1)}, bf16[1024,768]{1,0:T(8,128)(2,1)}, u32[]{:S(2)}) copy-start(bf16[1024,768]{1,0:T(8,128)(2,1)} %param.13) | copy-start | bytes 4718596
  6.5 204.9 %all-gather.13.cloned.1.call-start = ((), (), s32[]{:S(2)}) async-start(), calls=%async_computation.4 | async-start | bytes 17039360 | tf_op jit(solution)/shard_map/all_gather | solution.py:18
  8.5 395.8 %all-gather.9.cloned.1.call-start = ((), (), s32[]{:S(2)}) async-start(), calls=%async_computation.2 | async-start | bytes 17039360 | tf_op jit(solution)/shard_map/all_gather | solution.py:18
  9.2 451.4 %all-gather.15.cloned.1.call-start = ((), (), s32[]{:S(2)}) async-start(), calls=%async_computation.5 | async-start | bytes 2359296 | tf_op jit(solution)/shard_map/all_gather | solution.py:40
  220.9 192.9 %copy-start.6 = (s32[1,1024]{1,0:T(1,128)S(1)}, s32[1,1024]{1,0:T(1,128)}, u32[]{:S(2)}) copy-start(s32[1,1024]{1,0:T(1,128)} %param.12) | copy-start | bytes 12292
  220.9 195.8 %copy-start.10 = (s32[2]{0:T(128)S(1)}, s32[2]{0:T(128)}, u32[]{:S(2)}) copy-start(s32[2]{0:T(128)} %constant.68) | copy-start | bytes 28
  220.9 195.9 %copy-start.9 = (s32[2]{0:T(128)S(1)}, s32[2]{0:T(128)}, u32[]{:S(2)}) copy-start(s32[2]{0:T(128)} %constant.71) | copy-start | bytes 28
  220.9 204.9 %copy-start.5 = (bf16[1,152,4096]{2,1,0:T(8,128)(2,1)S(1)}, bf16[1,152,4096]{2,1,0:T(8,128)(2,1)}, u32[]{:S(2)}) copy-start(bf16[1,152,4096]{2,1,0:T(8,128)(2,1)} %param.8) | copy-start | bytes 3735556
  220.9 300.8 %all-gather.11.cloned.1.call-start = ((), (), s32[]{:S(2)}) async-start(), calls=%async_computation.3 | async-start | bytes 2359296 | tf_op jit(solution)/shard_map/all_gather | solution.py:40
  421.8 137.8 %all-to-all-start = ((s32[8,1,256]{2,1,0:T(1,128)}), s32[8,1,256]{2,1,0:T(1,128)S(1)}, u32[]{:S(2)}, u32[]{:S(2)}) async-start(s32[8,1,256]{2,1,0:T(1,128)} %bitcast.6), calls=%async_computation | async-start | bytes 16384 | tf_op jit(solution)/shard_map/all_to_all | solution.py:66
  429.9 5.2 copy-start.8
  525.9 3.4 copy-start.2
  525.9 3.9 copy-start.4
  529.8 1.7 copy-start.3
  531.5 1.7 copy-start.1
  533.2 0.8 copy-start.7
  559.6 30.5 %all-to-all-start.1 = ((bf16[8,256,512]{2,1,0:T(8,128)(2,1)}), bf16[8,256,512]{2,1,0:T(8,128)(2,1)}, u32[]{:S(2)}, u32[]{:S(2)}) async-start(bf16[8,256,512]{2,1,0:T(8,128)(2,1)} %bitcast.75), calls=%async_computation.1 | async-start | bytes 4194304 | tf_op jit(solution)/shard_map/all_to_all | solution.py:65
Sparse Core Ops, SparseCore 0:
  10.6 200.7 all-gather.12
  214.7 189.5 all-gather.8
  406.4 54.2 all-gather.14
  462.6 59.1 all-gather.10
